TPU v7x, 512 devices: a whole 4x8x8 slice. The times are simulated.
512 devices in a mesh: tile: 256 (over z, y, x), filt: 2 (over core).
Axes of the slice: x: 4, y: 8, z: 8, core: 2. Of those that a mesh axis runs over, the one named last changes fastest.
Arguments:
- coarse: bfloat16 [256, 8, 16, 320], P('tile', None, None, 'filt'), may hold values from -6 to 6
- up_weight: bfloat16 [256, 20480], P('filt'), may hold values from -0.125 to 0.125
- up_bias: bfloat16 [256], P('filt'), may hold values from -3 to 3
- mix_weight: bfloat16 [27, 256, 256], P(None, 'filt'), may hold values from -0.078125 to 0.078125
- mix_bias: bfloat16 [256], P('filt'), may hold values from -3 to 3
Outputs:
- fine: bfloat16 [512, 16, 32, 256], P('tile', None, None, 'filt')
All inputs are finite; a program needn't handle non-finite values.
Results may differ from a plain program's by a relative error of at most 0.0045.
Values may be sent and summed in bfloat16 or wider, within the bound.
A program may use at most 64 MiB of HBM per device.

v0:
```python
import jax
import jax.numpy as jnp
from jax import lax
from jax.sharding import PartitionSpec as P


def with_halo(block, sides, width):
    for axis, dim in sides:
        count = lax.axis_size(axis)
        forward = [(i, i + 1) for i in range(count - 1)]
        backward = [(target, source) for source, target in forward]
        low = lax.ppermute(
            lax.slice_in_dim(block, block.shape[dim] - width, None, axis=dim), axis, forward
        )
        high = lax.ppermute(lax.slice_in_dim(block, 0, width, axis=dim), axis, backward)
        block = jnp.concatenate([low, block, high], axis=dim)
    return block


def upsample_piece(total, piece, kernel, extra):
    padded = jnp.pad(piece, ((extra, extra), (1, 1), (1, 1), (0, 0)))
    rows_y = padded.shape[0] - 2
    rows_z = piece.shape[1]
    rows_x = piece.shape[2]
    results = []
    for odd_y in (0, 1):
        for odd_x in (0, 1):
            for odd_z in (0, 1):
                partial_sum = total[odd_y, odd_x, odd_z]
                for tap_y in (0, 1):
                    for tap_x in (0, 1):
                        for tap_z in (0, 1):
                            start_y = odd_y + tap_y
                            start_x = odd_x + tap_x
                            start_z = odd_z + tap_z
                            window = padded[
                                start_y : start_y + rows_y,
                                start_z : start_z + rows_z,
                                start_x : start_x + rows_x,
                                :,
                            ]
                            taps = kernel[
                                :,
                                3 - odd_y - 2 * tap_y,
                                3 - odd_x - 2 * tap_x,
                                3 - odd_z - 2 * tap_z,
                            ]
                            partial_sum = partial_sum + jnp.einsum(
                                "yzxc,fc->yzxf", window, taps, preferred_element_type=jnp.float32
                            )
                results.append(partial_sum)
    return jnp.stack(results).reshape(total.shape)


def mix_sum(total, padded, weight):
    rows_y, rows_z, rows_x = (total.shape[0], total.shape[1], total.shape[2])
    for shift_y in range(3):
        for shift_x in range(3):
            for shift_z in range(3):
                window = padded[
                    shift_y : shift_y + rows_y,
                    shift_z : shift_z + rows_z,
                    shift_x : shift_x + rows_x,
                    :,
                ]
                taps = weight[9 * shift_y + 3 * shift_x + shift_z]
                total = total + jnp.einsum(
                    "yzxc,fc->yzxf", window, taps, preferred_element_type=jnp.float32
                )
    return total


def local(coarse, up_weight, up_bias, mix_weight, mix_bias):
    low_rows, low_z, low_x = (coarse.shape[0], coarse.shape[1], coarse.shape[2])
    out_local = up_weight.shape[0]
    kernel = up_weight.reshape(out_local, 4, 4, 4, up_weight.shape[1] // 64)
    extended = with_halo(coarse, (("tile", 0),), 1)
    extra = 0
    coarse_rows = low_rows + 2 * extra
    empty = jnp.zeros((2, 2, 2, coarse_rows, low_z, low_x, out_local), jnp.float32)
    upsampled = upsample_piece(
        empty, lax.all_gather(extended, "filt", axis=3, tiled=True), kernel, extra
    )
    upsampled = jnp.transpose(upsampled, (3, 0, 4, 2, 5, 1, 6)).reshape(
        2 * coarse_rows, 2 * low_z, 2 * low_x, out_local
    )
    hidden = (upsampled + up_bias.astype(jnp.float32)).astype(jnp.bfloat16)
    hidden_ext = with_halo(hidden, (("tile", 0),), 1)
    rows_y = hidden_ext.shape[0] - 2
    rows_z, rows_x = (hidden_ext.shape[1], hidden_ext.shape[2])
    start_total = jnp.zeros((rows_y, rows_z, rows_x, out_local), jnp.float32)
    padded = jnp.pad(
        lax.all_gather(hidden_ext, "filt", axis=3, tiled=True), ((0, 0), (1, 1), (1, 1), (0, 0))
    )
    mixed = mix_sum(start_total, padded, mix_weight)
    fine = jnp.maximum(mixed + mix_bias.astype(jnp.float32), 0.0).astype(jnp.bfloat16)
    return fine


def solution(mesh):
    placed = (
        P("tile", None, None, "filt"),
        P("filt", None),
        P("filt"),
        P(None, "filt", None),
        P("filt"),
    )
    return jax.shard_map(
        local, mesh=mesh, in_specs=placed, out_specs=P("tile", None, None, "filt"), check_vma=False
    )
```

profile of v0, /device:TPU:1, one launch (start us, length us, event | category | flops | bytes accessed | tf_op | source)
XLA Modules:
  0.0 115.4 jit_solution(17227349220186519037)
XLA Ops:
  6.5 1.4 %collective-permute-start.1 = (bf16[1,8,16,160]{3,2,1,0:T(8,128)(2,1)}, bf16[1,8,16,160]{3,2,1,0:T(8,128)(2,1)S(1)}, u32[]{:S(2)}, u32[]{:S(2)}) collective-permute-start(bf16[1,8,16,160]{3,2,1,0:T(8,128)(2,1)} %param.5), channel_id=1, source_target_pairs={{2,0},{4,2},{6,4},{8,6},{10,8},{12,10},{14,12},{16,14},{18,16},{20... | collective-permute-start | bytes 122888 | tf_op jit(solution)/shard_map/ppermute | solution.py:15
  8.0 4.6 %collective-permute-start = (bf16[1,8,16,160]{3,2,1,0:T(8,128)(2,1)}, bf16[1,8,16,160]{3,2,1,0:T(8,128)(2,1)S(1)}, u32[]{:S(2)}, u32[]{:S(2)}) collective-permute-start(bf16[1,8,16,160]{3,2,1,0:T(8,128)(2,1)} %param.5), channel_id=1, source_target_pairs={{0,2},{2,4},{4,6},{6,8},{8,10},{10,12},{12,14},{14,16},{16,18},{18... | collective-permute-start | bytes 122888 | tf_op jit(solution)/shard_map/ppermute | solution.py:12
  12.5 8.1 %copy.19 = bf16[128,20480]{0,1:T(8,128)(2,1)} copy(bf16[128,20480]{1,0:T(8,128)(2,1)} %param.6) | data formatting | bytes 10485760 | tf_op args[1]
  21.2 9.7 %all_gather.6 = bf16[3,8,16,320]{2,1,0,3:T(8,128)(2,1)S(1)} all-gather(bf16[3,8,16,160]{2,1,0,3:T(8,128)(2,1)S(1)} %copy.17), channel_id=1, replica_groups=mesh['tile'=256,'filt'=2] {'filt'}, dimensions={3}, use_global_device_ids=true | all-gather | bytes 368640 | tf_op jit(solution)/shard_map/all_gather | solution.py:82
  30.9 2.7 %copy.18 = bf16[3,8,16,320]{3,2,1,0:T(8,128)(2,1)S(1)} copy(bf16[3,8,16,320]{2,1,0,3:T(8,128)(2,1)S(1)} %all_gather.6) | data formatting | bytes 491520 | tf_op jit(solution)/shard_map/all_gather | solution.py:82
  33.6 1.2 %fusion.60 = f32[8,16,128]{2,1,0:T(8,128)S(1)} fusion(bf16[3,8,16,320]{3,2,1,0:T(8,128)(2,1)S(1)} %copy.18, bf16[128,4,4,4,320]{0,4,3,2,1:T(8,128)(2,1)} %bitcast.667), kind=kOutput, calls=%fused_computation.183 | convolution fusion | flops 10485760 | bytes 393216 | tf_op jit(solution)/shard_map/yzxc,fc->yzxf/dot_general | solution.py:48
  34.8 1.4 %fusion.68 = f32[8,16,128]{2,1,0:T(8,128)S(1)} fusion(bf16[128,4,4,4,320]{0,4,3,2,1:T(8,128)(2,1)} %bitcast.668, bf16[3,8,16,320]{3,2,1,0:T(8,128)(2,1)S(1)} %copy.18), kind=kOutput, calls=%fused_computation.246 | convolution fusion | flops 10485760 | bytes 393216 | tf_op jit(solution)/shard_map/yzxc,fc->yzxf/dot_general | solution.py:48
  36.2 1.1 fusion.67
  37.3 1.0 fusion.66
  38.3 1.1 fusion.65
  39.4 1.0 fusion.64
  40.4 1.1 fusion.63
  41.5 1.0 fusion.62
  42.5 1.0 convolution_add_fusion.75
  43.6 1.1 convolution_add_fusion.74
  44.6 1.0 convolution_add_fusion.73
  45.7 1.1 convolution_add_fusion.72
  46.8 1.0 convolution_add_fusion.71
  47.8 1.1 convolution_add_fusion.70
  48.9 1.0 fusion.24
  49.9 1.1 convolution_add_fusion.68
  59.7 1.3 %collective-permute-start.3 = (bf16[1,16,32,128]{3,2,1,0:T(8,128)(2,1)S(1)}, bf16[1,16,32,128]{3,2,1,0:T(8,128)(2,1)S(1)}, u32[]{:S(2)}, u32[]{:S(2)}) collective-permute-start(bf16[1,16,32,128]{3,2,1,0:T(8,128)(2,1)S(1)} %get-tuple-element.6), channel_id=1, source_target_pairs={{2,0},{4,2},{6,4},{8,6},{10,8},{12,10},{14,12},{16,14},{18,16},{20... | collective-permute-start | bytes 393224 | tf_op jit(solution)/shard_map/ppermute | solution.py:15
  61.0 4.2 %collective-permute-start.2 = (bf16[1,16,32,128]{3,2,1,0:T(8,128)(2,1)S(1)}, bf16[1,16,32,128]{3,2,1,0:T(8,128)(2,1)S(1)}, u32[]{:S(2)}, u32[]{:S(2)}) collective-permute-start(bf16[1,16,32,128]{3,2,1,0:T(8,128)(2,1)S(1)} %get-tuple-element.5), channel_id=1, source_target_pairs={{0,2},{2,4},{4,6},{6,8},{8,10},{10,12},{12,14},{14,16},{16,18},{18... | collective-permute-start | bytes 393224 | tf_op jit(solution)/shard_map/ppermute | solution.py:12
  65.2 1.1 collective-permute-done.3
  66.3 0.9 collective-permute-done.2
  67.1 0.9 pad_maximum_fusion
  68.1 27.2 %all-gather.2.cloned.1.call-done = bf16[4,16,32,256]{3,2,1,0:T(8,128)(2,1)} async-done(((bf16[4,16,32,128]{3,2,1,0:T(8,128)(2,1)}), bf16[4,16,32,256]{3,2,1,0:T(8,128)(2,1)}) %all-gather.2.cloned.1.call-update) | async-done | bytes 1048592 | tf_op jit(solution)/shard_map/all_gather | solution.py:93
  95.3 1.4 %fusion.28 = f32[2,16,32,128]{3,2,1,0:T(8,128)S(1)} fusion(bf16[4,16,32,256]{3,2,1,0:T(8,128)(2,1)} %all-gather.2.cloned.1.call-done, bf16[27,128,256]{2,1,0:T(8,128)(2,1)S(1)} %copy-done.2), kind=kOutput, calls=%fused_computation.152 | convolution fusion | flops 67108864 | bytes 1638400 | tf_op jit(solution)/shard_map/yzxc,fc->yzxf/dot_general | solution.py:67
  96.7 1.3 %fusion.73 = f32[2,16,32,128]{3,2,1,0:T(8,128)S(1)} fusion(bf16[4,16,32,256]{3,2,1,0:T(8,128)(2,1)} %all-gather.2.cloned.1.call-done, bf16[27,128,256]{2,1,0:T(8,128)(2,1)S(1)} %copy-done.2), kind=kOutput, calls=%fused_computation.259 | convolution fusion | flops 67108864 | bytes 1638400 | tf_op jit(solution)/shard_map/yzxc,fc->yzxf/dot_general | solution.py:67
  98.0 1.3 %fusion.27 = f32[2,16,32,128]{3,2,1,0:T(8,128)S(1)} fusion(bf16[4,16,32,256]{3,2,1,0:T(8,128)(2,1)} %all-gather.2.cloned.1.call-done, bf16[27,128,256]{2,1,0:T(8,128)(2,1)S(1)} %copy-done.2), kind=kOutput, calls=%fused_computation.151 | convolution fusion | flops 67108864 | bytes 1638400 | tf_op jit(solution)/shard_map/yzxc,fc->yzxf/dot_general | solution.py:67
  99.3 1.3 %fusion.83 = f32[2,16,32,128]{3,2,1,0:T(8,128)S(1)} fusion(bf16[4,16,32,256]{3,2,1,0:T(8,128)(2,1)} %all-gather.2.cloned.1.call-done, bf16[27,128,256]{2,1,0:T(8,128)(2,1)S(1)} %copy-done.2), kind=kOutput, calls=%fused_computation.269 | convolution fusion | flops 67108864 | bytes 1638400 | tf_op jit(solution)/shard_map/yzxc,fc->yzxf/dot_general | solution.py:67
  107.6 1.0 fusion.8
  (93 shorter events, 15.7 us)
Async XLA Ops:
  6.5 14.1 %copy-start.3 = (bf16[1,8,16,160]{3,2,1,0:T(8,128)(2,1)S(1)}, bf16[1,8,16,160]{3,2,1,0:T(8,128)(2,1)}, u32[]{:S(2)}) copy-start(bf16[1,8,16,160]{3,2,1,0:T(8,128)(2,1)} %param.5) | copy-start | bytes 122884
  6.5 14.1 %copy-start.4 = (bf16[128]{0:T(256)(128)(2,1)S(1)}, bf16[128]{0:T(256)(128)(2,1)}, u32[]{:S(2)}) copy-start(bf16[128]{0:T(256)(128)(2,1)} %param.7) | copy-start | bytes 772
  6.5 88.7 %all-gather.2.cloned.1.call-start = ((), (), s32[]{:S(2)}) async-start(), calls=%async_computation | async-start | bytes 1572864 | tf_op jit(solution)/shard_map/all_gather | solution.py:93
  6.5 14.1 %collective-permute-start.1 = (bf16[1,8,16,160]{3,2,1,0:T(8,128)(2,1)}, bf16[1,8,16,160]{3,2,1,0:T(8,128)(2,1)S(1)}, u32[]{:S(2)}, u32[]{:S(2)}) collective-permute-start(bf16[1,8,16,160]{3,2,1,0:T(8,128)(2,1)} %param.5), channel_id=1, source_target_pairs={{2,0},{4,2},{6,4},{8,6},{10,8},{12,10},{14,12},{16,14},{18,16},{20... | collective-permute-start | bytes 122888 | tf_op jit(solution)/shard_map/ppermute | solution.py:15
  8.0 12.7 %collective-permute-start = (bf16[1,8,16,160]{3,2,1,0:T(8,128)(2,1)}, bf16[1,8,16,160]{3,2,1,0:T(8,128)(2,1)S(1)}, u32[]{:S(2)}, u32[]{:S(2)}) collective-permute-start(bf16[1,8,16,160]{3,2,1,0:T(8,128)(2,1)} %param.5), channel_id=1, source_target_pairs={{0,2},{2,4},{4,6},{6,8},{8,10},{10,12},{12,14},{14,16},{16,18},{18... | collective-permute-start | bytes 122888 | tf_op jit(solution)/shard_map/ppermute | solution.py:12
  33.6 17.4 %copy-start.1 = (bf16[128,20480]{0,1:T(8,128)(2,1)S(1)}, bf16[128,20480]{0,1:T(8,128)(2,1)}, u32[]{:S(2)}) copy-start(bf16[128,20480]{0,1:T(8,128)(2,1)} %copy.19) | copy-start | bytes 15728644
  56.8 11.3 %copy-start.5 = (bf16[128]{0:T(256)(128)(2,1)S(1)}, bf16[128]{0:T(256)(128)(2,1)}, u32[]{:S(2)}) copy-start(bf16[128]{0:T(256)(128)(2,1)} %param.9) | copy-start | bytes 772
  56.8 38.5 %copy-start.2 = (bf16[27,128,256]{2,1,0:T(8,128)(2,1)S(1)}, bf16[27,128,256]{2,1,0:T(8,128)(2,1)}, u32[]{:S(2)}) copy-start(bf16[27,128,256]{2,1,0:T(8,128)(2,1)} %param.8) | copy-start | bytes 5308420
  59.7 6.6 %collective-permute-start.3 = (bf16[1,16,32,128]{3,2,1,0:T(8,128)(2,1)S(1)}, bf16[1,16,32,128]{3,2,1,0:T(8,128)(2,1)S(1)}, u32[]{:S(2)}, u32[]{:S(2)}) collective-permute-start(bf16[1,16,32,128]{3,2,1,0:T(8,128)(2,1)S(1)} %get-tuple-element.6), channel_id=1, source_target_pairs={{2,0},{4,2},{6,4},{8,6},{10,8},{12,10},{14,12},{16,14},{18,16},{20... | collective-permute-start | bytes 393224 | tf_op jit(solution)/shard_map/ppermute | solution.py:15
  61.0 6.2 %collective-permute-start.2 = (bf16[1,16,32,128]{3,2,1,0:T(8,128)(2,1)S(1)}, bf16[1,16,32,128]{3,2,1,0:T(8,128)(2,1)S(1)}, u32[]{:S(2)}, u32[]{:S(2)}) collective-permute-start(bf16[1,16,32,128]{3,2,1,0:T(8,128)(2,1)S(1)} %get-tuple-element.5), channel_id=1, source_target_pairs={{0,2},{2,4},{4,6},{6,8},{8,10},{10,12},{12,14},{14,16},{16,18},{18... | collective-permute-start | bytes 393224 | tf_op jit(solution)/shard_map/ppermute | solution.py:12
  95.3 5.4 %copy-start = (bf16[4,16,32,256]{3,2,1,0:T(8,128)(2,1)S(1)}, bf16[4,16,32,256]{3,2,1,0:T(8,128)(2,1)}, u32[]{:S(2)}) copy-start(bf16[4,16,32,256]{3,2,1,0:T(8,128)(2,1)} %all-gather.2.cloned.1.call-done) | copy-start | bytes 3145732
Sparse Core Ops, SparseCore 0:
  68.2 27.0 all-gather.1
where the time goes:
time: 117 us; the launch traced here: 115 us
  matrix products  38.3 us (33%)
  waiting for transfers between devices  29.2 us (25%)
  between operations  14.1 us (12%)
  local copies, waits for them, and re-layouts  11.7 us (10%)
  starting transfers between devices  11.5 us (10%)
  blocking collectives  9.69 us (8%)
    all_gather x1, waiting for transfers between devices, local(): lax.all_gather(hidden_ext, 'filt', axis=3, tiled=True)  27.2 us
    dot_general x64, matrix products, upsample_piece(): jnp.einsum('yzxc,fc->yzxf', window, taps, preferred_element_type=jnp.floa...  25.1 us
    dot_general x27, matrix products, mix_sum(): jnp.einsum('yzxc,fc->yzxf', window, taps, preferred_element_type=jnp.floa...  13.2 us
    all_gather x1, blocking collectives, local(): lax.all_gather(extended, 'filt', axis=3, tiled=True)  9.69 us
    ppermute x2, starting transfers between devices, with_halo(): lax.ppermute(lax.slice_in_dim(block, block.shape[dim] - width, None, axis...  8.75 us
    unnamed x13, local copies, waits for them, and re-layouts  8.12 us
    ppermute x2, starting transfers between devices, with_halo(): lax.ppermute(lax.slice_in_dim(block, 0, width, axis=dim), axis, backward)  2.7 us
    all_gather x1, local copies, waits for them, and re-layouts, local(): lax.all_gather(extended, 'filt', axis=3, tiled=True)  2.67 us
  transfers between devices with their start and end apart: 5, of which 3 were waited for; matrix products, arithmetic and copies ran while one was open for 7% of the time, Pallas kernels for 0%

commit v1 on v0

v1 whole, which is shorter than its diff:
```python
import jax
import jax.numpy as jnp
from jax import lax
from jax.experimental import pallas as pl
from jax.experimental.pallas import tpu as pltpu
from jax.sharding import PartitionSpec as P

MESH = pl.DeviceIdType.MESH
NT = (((1,), (1,)), ((), ()))

TAPS = (((-1, 3), (0, 1)), ((0, 2), (1, 0)))


def dot_nt(a, b):
    return lax.dot_general(a, b, NT, preferred_element_type=jnp.float32)


def kernel(
    coarse, upw, upb, mixw, mixb, out,
    cbuf, wup, wmix, ub, mb, xb, hid, scr,
    up_sem, mix_sem, bias_sem, own_sem, send_sem, recv_sem, hsend, hrecv,
):
    tiles = lax.axis_size("tile")
    t = lax.axis_index("tile")
    c = lax.axis_index("filt")
    other = 1 - c
    right = lax.rem(t + 1, tiles)
    left = lax.rem(t + tiles - 1, tiles)
    zl, xl, cs = coarse.shape[1:]
    f = upw.shape[0]
    cin = 2 * cs
    targets = ((t, other), (right, c), (right, other), (left, c), (left, other))
    slots = (1, 0, 0, 2, 2)

    barrier = pltpu.get_barrier_semaphore()
    for dev in targets:
        pl.semaphore_signal(barrier, inc=1, device_id=dev, device_id_type=MESH)

    own_copy = pltpu.make_async_copy(coarse.at[0], cbuf.at[1, c], own_sem)
    own_copy.start()
    bias_copies = [
        pltpu.make_async_copy(upb, ub, bias_sem.at[0]),
        pltpu.make_async_copy(mixb, mb, bias_sem.at[1]),
    ]
    for copy in bias_copies:
        copy.start()
    up_copies = {}
    for px in (0, 1):
        for _, kx in TAPS[px]:
            for ky in range(4):
                cols = pl.ds((16 * ky + 4 * kx) * cin, 4 * cin)
                copy = pltpu.make_async_copy(
                    upw.at[:, cols], wup.at[:, cols], up_sem.at[4 * ky + kx]
                )
                copy.start()
                up_copies[ky, kx] = copy
    mix_copies = []
    for half, src in ((0, c), (1, other)):
        copy = pltpu.make_async_copy(
            mixw.at[:, :, pl.ds(pl.multiple_of(src * f, f), f)], wmix.at[half], mix_sem.at[half]
        )
        copy.start()
        mix_copies.append(copy)

    xb[:, :, :, 0] = jnp.zeros_like(xb[:, :, :, 0])
    xb[:, :, :, zl + 1] = jnp.zeros_like(xb[:, :, :, zl + 1])
    hid[:, :, 0] = jnp.zeros_like(hid[:, :, 0])
    hid[:, :, 2 * zl + 1] = jnp.zeros_like(hid[:, :, 2 * zl + 1])

    pl.semaphore_wait(barrier, 5)
    sends = []
    for k, (dev, slot) in enumerate(zip(targets, slots)):
        copy = pltpu.make_async_remote_copy(
            src_ref=coarse.at[0],
            dst_ref=cbuf.at[slot, c],
            send_sem=send_sem.at[k],
            recv_sem=recv_sem.at[k],
            device_id=dev,
            device_id_type=MESH,
        )
        copy.start()
        sends.append(copy)

    first = (t > 0).astype(jnp.float32)
    last = (t < tiles - 1).astype(jnp.float32)

    def place(slot, scale):
        x = cbuf[slot].astype(jnp.float32)
        x = jnp.concatenate([x[0], x[1]], axis=-1)
        if scale is not None:
            x = x * scale
        gap = jnp.zeros((zl, xl, 64), jnp.float32)
        edge = jnp.zeros((zl, 1, cin + 64), jnp.float32)
        for v, parts in enumerate(([gap, x], [x, gap])):
            y = jnp.concatenate(parts, axis=-1)
            low = jnp.concatenate([edge, y[:, :-1]], axis=1)
            high = jnp.concatenate([y[:, 1:], edge], axis=1)
            for s, w in enumerate((low, y, high)):
                xb[v, s, slot, 1 : zl + 1] = w.astype(jnp.bfloat16)

    own_copy.wait()
    sends[0].wait_recv()
    place(1, None)
    sends[1].wait_recv()
    sends[2].wait_recv()
    place(0, first)
    sends[3].wait_recv()
    sends[4].wait_recv()
    place(2, last)

    for copy in bias_copies:
        copy.wait()
    ubias = ub[...].astype(jnp.float32).reshape(1, 1, 1, f)
    mbias = mb[...].astype(jnp.float32).reshape(1, f)

    m = 2 * zl * xl
    swaps = []
    for px in (0, 1):
        for _, kx in TAPS[px]:
            for ky in range(4):
                up_copies[ky, kx].wait()
        for pz in (0, 1):
            lhs, even, odd = [], [], []
            for yt in (0, 1):
                for dz, kz in TAPS[pz]:
                    for dx, kx in TAPS[px]:
                        lhs.append(
                            xb[pz, dx + 1, yt : yt + 2, dz + 1 : dz + 1 + zl].reshape(m, cin + 64)
                        )
                        for ky, group in ((2 - 2 * yt, even), (3 - 2 * yt, odd)):
                            start = (16 * ky + 4 * kx + kz) * cin - (0 if pz else 64)
                            group.append(wup[:, start : start + cin + 64])
            rhs = jnp.concatenate(
                [jnp.concatenate(even, axis=1), jnp.concatenate(odd, axis=1)], axis=0
            )
            up = dot_nt(jnp.concatenate(lhs, axis=1), rhs)
            for q in (0, 1):
                for j in (0, 1):
                    r = 2 * j + q
                    h = up[j * zl * xl : (j + 1) * zl * xl, q * f : (q + 1) * f]
                    h = h.reshape(zl, xl, f) + ubias[0]
                    if r == 0:
                        h = h * first
                    if r == 3:
                        h = h * last
                    edge = jnp.zeros((zl, 1, f), jnp.float32)
                    if px:
                        moved = jnp.concatenate([edge, h[:, :-1]], axis=1)
                    else:
                        moved = jnp.concatenate([h[:, 1:], edge], axis=1)
                    h = h.astype(jnp.bfloat16)
                    moved = moved.astype(jnp.bfloat16)
                    for i in range(zl):
                        zz = 1 + 2 * i + pz
                        hid[0, r, zz, :, (1 + px) * f : (2 + px) * f] = h[i]
                        lane = 0 if px else 3 * f
                        hid[0, r, zz, :, lane : lane + f] = moved[i]
        copy = pltpu.make_async_remote_copy(
            src_ref=hid.at[0, :, pl.ds(1, 2 * zl), :, pl.ds((1 + px) * f, f)],
            dst_ref=hid.at[1, :, pl.ds(1, 2 * zl), :, pl.ds((1 + px) * f, f)],
            send_sem=hsend.at[px],
            recv_sem=hrecv.at[px],
            device_id=(t, other),
            device_id_type=MESH,
        )
        copy.start()
        swaps.append(copy)

    def mix(half):
        lhs = [[], []]
        groups = [[], []]
        blank = jnp.zeros((f, 3 * f), jnp.bfloat16)
        for r in range(4):
            for dz in range(3):
                for p in (0, 1):
                    lhs[p].append(
                        hid[half, r, dz : dz + 2 * zl, :, p * f : (p + 3) * f].reshape(m, 3 * f)
                    )
                for a in (0, 1):
                    dy = r - a
                    if 0 <= dy < 3:
                        taps = [wmix[half, 9 * dy + 3 * dx + dz] for dx in range(3)]
                        groups[a].append(jnp.concatenate(taps, axis=1))
                    else:
                        groups[a].append(blank)
        rhs = jnp.concatenate([jnp.concatenate(g, axis=1) for g in groups], axis=0)
        left_side = jnp.concatenate([jnp.concatenate(g, axis=1) for g in lhs], axis=0)
        return dot_nt(left_side, rhs)

    mix_copies[0].wait()
    total = mix(0)
    for copy in swaps:
        copy.wait_recv()
    for px in (0, 1):
        for r in range(4):
            h = hid[1, r, 1 : 2 * zl + 1, :, (1 + px) * f : (2 + px) * f].astype(jnp.float32)
            edge = jnp.zeros((2 * zl, 1, f), jnp.float32)
            if px:
                moved = jnp.concatenate([edge, h[:, :-1]], axis=1)
            else:
                moved = jnp.concatenate([h[:, 1:], edge], axis=1)
            lane = 0 if px else 3 * f
            hid[1, r, 1 : 2 * zl + 1, :, lane : lane + f] = moved.astype(jnp.bfloat16)
    mix_copies[1].wait()
    total = total + mix(1)

    for a in (0, 1):
        for p in (0, 1):
            y = total[p * m : (p + 1) * m, a * f : (a + 1) * f] + mbias
            y = jnp.maximum(y, 0.0).reshape(2 * zl, xl, f)
            scr[:, pl.ds(p, xl, stride=2), :] = y
        out[a] = scr[...].astype(jnp.bfloat16)

    for copy in sends:
        copy.wait_send()
    for copy in swaps:
        copy.wait_send()


def local(coarse, up_weight, up_bias, mix_weight, mix_bias):
    _, zl, xl, cs = coarse.shape
    f = up_weight.shape[0]
    bf16 = jnp.bfloat16
    anywhere = pl.BlockSpec(memory_space=pl.ANY)
    return pl.pallas_call(
        kernel,
        out_shape=jax.ShapeDtypeStruct((2, 2 * zl, 2 * xl, f), bf16),
        in_specs=[anywhere] * 5,
        out_specs=pl.BlockSpec(memory_space=pltpu.VMEM),
        scratch_shapes=[
            pltpu.VMEM((3, 2, zl, xl, cs), bf16),
            pltpu.VMEM(up_weight.shape, bf16),
            pltpu.VMEM((2, 27, f, f), bf16),
            pltpu.VMEM((f,), bf16),
            pltpu.VMEM((f,), bf16),
            pltpu.VMEM((2, 3, 3, zl + 2, xl, 2 * cs + 64), bf16),
            pltpu.VMEM((2, 4, 2 * zl + 2, xl, 4 * f), bf16),
            pltpu.VMEM((2 * zl, 2 * xl, f), jnp.float32),
            pltpu.SemaphoreType.DMA((16,)),
            pltpu.SemaphoreType.DMA((2,)),
            pltpu.SemaphoreType.DMA((2,)),
            pltpu.SemaphoreType.DMA,
            pltpu.SemaphoreType.DMA((5,)),
            pltpu.SemaphoreType.DMA((5,)),
            pltpu.SemaphoreType.DMA((2,)),
            pltpu.SemaphoreType.DMA((2,)),
        ],
        compiler_params=pltpu.CompilerParams(
            collective_id=0, has_side_effects=True, vmem_limit_bytes=60 * 1024 * 1024
        ),
        cost_estimate=pl.CostEstimate(
            flops=2_500_000_000, bytes_accessed=8_000_000, transcendentals=0
        ),
        name="section",
    )(coarse, up_weight, up_bias, mix_weight, mix_bias)


def solution(mesh):
    placed = (
        P("tile", None, None, "filt"),
        P("filt", None),
        P("filt"),
        P(None, "filt", None),
        P("filt"),
    )
    return jax.shard_map(
        local, mesh=mesh, in_specs=placed, out_specs=P("tile", None, None, "filt"), check_vma=False
    )
```

time: 117 us -> 29.9 us (0.26); the launches traced: 115 us -> 29.7 us
  matrix products: 38.3 us -> 0 us
  waiting for transfers between devices: 29.2 us -> 0 us
  Pallas kernels: 0 us -> 28.1 us
  between operations: 14.1 us -> 0.01 us
  starting transfers between devices: 11.5 us -> 0 us
  local copies, waits for them, and re-layouts: 11.7 us -> 1.67 us
  blocking collectives: 9.69 us -> 0 us
    dot_general x91 -> x0, matrix products: 38.3 us -> none  [the longest x64 25.1 us: upsample_piece(): jnp.einsum('yzxc,fc->yzxf', window, taps, preferred_element_type=jnp.floa...]
    pallas_call x0 -> x1, Pallas kernels: none -> 28.1 us  [local(): pl.pallas_call(kernel, out_shape=jax.ShapeDtypeStruct((2, 2 * zl, 2 * xl,...]
    all_gather x1 -> x0, waiting for transfers between devices: 27.2 us -> none  [local(): lax.all_gather(hidden_ext, 'filt', axis=3, tiled=True)]
    ppermute x4 -> x0, starting transfers between devices: 11.5 us -> none  [the longest x2 8.75 us: with_halo(): lax.ppermute(lax.slice_in_dim(block, block.shape[dim] - width, None, axis...]
    all_gather x1 -> x0, blocking collectives: 9.69 us -> none  [local(): lax.all_gather(extended, 'filt', axis=3, tiled=True)]
    unnamed x13 -> x1, local copies, waits for them, and re-layouts: 8.12 us -> 1.67 us
    all_gather x1 -> x0, local copies, waits for them, and re-layouts: 2.67 us -> none  [local(): lax.all_gather(extended, 'filt', axis=3, tiled=True)]
    ppermute x4 -> x0, waiting for transfers between devices: 1.98 us -> none  [the longest x2 1.12 us: with_halo(): lax.ppermute(lax.slice_in_dim(block, 0, width, axis=dim), axis, backward)]
  transfers between devices with their start and end apart: 5 -> 0, of which waited for: 3 -> 0; matrix products, arithmetic and copies ran while one was open for 7% -> 0% of each run, Pallas kernels for 0% -> 0%
where the time goes in v1:
time: 29.9 us; the launch traced here: 29.7 us
  Pallas kernels  28.1 us (94%)
  local copies, waits for them, and re-layouts  1.67 us (6%)
    pallas_call x1, Pallas kernels, local(): pl.pallas_call(kernel, out_shape=jax.ShapeDtypeStruct((2, 2 * zl, 2 * xl,...  28.1 us
    unnamed x1, local copies, waits for them, and re-layouts  1.67 us

profile of v1, /device:TPU:1, one launch (start us, length us, event | category | flops | bytes accessed | tf_op | source)
XLA Modules:
  0.0 29.7 jit_solution(16452061528238032330)
XLA Ops:
  0.0 28.1 %section.1 = bf16[2,16,32,128]{3,2,1,0:T(8,128)(2,1)} custom-call(bf16[1,8,16,160]{3,2,1,0:T(8,128)(2,1)} %coarse.1, bf16[128,20480]{1,0:T(8,128)(2,1)} %upw.1, bf16[128]{0:T(256)(128)(2,1)} %upb.1, bf16[27,128,256]{2,1,0:T(8,128)(2,1)} %mixw.1, bf16[128]{0:T(256)(128)(2,1)} %mixb.1), custom_call_target="tpu_custom_call" | custom-call | flops 2500000000 | bytes 8000000 | tf_op jit(solution)/shard_map/section/pallas_call | solution.py:225
  28.1 1.7 %copy.7 = bf16[2,16,32,128]{3,2,1,0:T(8,128)(2,1)} copy(bf16[2,16,32,128]{3,2,1,0:T(8,128)(2,1)} %section.1) | data formatting | bytes 524288

commit v2 on v1

--- a/solution.py
+++ b/solution.py
@@ -24,17 +24,36 @@
     t = lax.axis_index("tile")
     c = lax.axis_index("filt")
     other = 1 - c
-    right = lax.rem(t + 1, tiles)
-    left = lax.rem(t + tiles - 1, tiles)
+    right = t + 1
+    left = t - 1
     zl, xl, cs = coarse.shape[1:]
     f = upw.shape[0]
     cin = 2 * cs
     targets = ((t, other), (right, c), (right, other), (left, c), (left, other))
     slots = (1, 0, 0, 2, 2)
 
+    has_left = t > 0
+    has_right = t < tiles - 1
+
+    def each(action):
+        action(0)
+
+        @pl.when(has_right)
+        def _():
+            action(1)
+            action(2)
+
+        @pl.when(has_left)
+        def _():
+            action(3)
+            action(4)
+
     barrier = pltpu.get_barrier_semaphore()
-    for dev in targets:
-        pl.semaphore_signal(barrier, inc=1, device_id=dev, device_id_type=MESH)
+    each(
+        lambda k: pl.semaphore_signal(
+            barrier, inc=1, device_id=targets[k], device_id_type=MESH
+        )
+    )
 
     own_copy = pltpu.make_async_copy(coarse.at[0], cbuf.at[1, c], own_sem)
     own_copy.start()
@@ -67,10 +86,19 @@
     hid[:, :, 0] = jnp.zeros_like(hid[:, :, 0])
     hid[:, :, 2 * zl + 1] = jnp.zeros_like(hid[:, :, 2 * zl + 1])
 
-    pl.semaphore_wait(barrier, 5)
-    sends = []
-    for k, (dev, slot) in enumerate(zip(targets, slots)):
-        copy = pltpu.make_async_remote_copy(
+    @pl.when(jnp.logical_not(has_left))
+    def _():
+        cbuf[0] = jnp.zeros_like(cbuf[0])
+
+    @pl.when(jnp.logical_not(has_right))
+    def _():
+        cbuf[2] = jnp.zeros_like(cbuf[2])
+
+    first = has_left.astype(jnp.int32)
+    last = has_right.astype(jnp.int32)
+    pl.semaphore_wait(barrier, 1 + 2 * first + 2 * last)
+    sends = [
+        pltpu.make_async_remote_copy(
             src_ref=coarse.at[0],
             dst_ref=cbuf.at[slot, c],
             send_sem=send_sem.at[k],
@@ -78,17 +106,15 @@
             device_id=dev,
             device_id_type=MESH,
         )
-        copy.start()
-        sends.append(copy)
-
-    first = (t > 0).astype(jnp.float32)
-    last = (t < tiles - 1).astype(jnp.float32)
-
-    def place(slot, scale):
+        for k, (dev, slot) in enumerate(zip(targets, slots))
+    ]
+    each(lambda k: sends[k].start())
+    first = first.astype(jnp.float32)
+    last = last.astype(jnp.float32)
+
+    def place(slot):
         x = cbuf[slot].astype(jnp.float32)
         x = jnp.concatenate([x[0], x[1]], axis=-1)
-        if scale is not None:
-            x = x * scale
         gap = jnp.zeros((zl, xl, 64), jnp.float32)
         edge = jnp.zeros((zl, 1, cin + 64), jnp.float32)
         for v, parts in enumerate(([gap, x], [x, gap])):
@@ -100,13 +126,21 @@
 
     own_copy.wait()
     sends[0].wait_recv()
-    place(1, None)
-    sends[1].wait_recv()
-    sends[2].wait_recv()
-    place(0, first)
-    sends[3].wait_recv()
-    sends[4].wait_recv()
-    place(2, last)
+    place(1)
+
+    @pl.when(has_left)
+    def _():
+        sends[1].wait_recv()
+        sends[2].wait_recv()
+
+    place(0)
+
+    @pl.when(has_right)
+    def _():
+        sends[3].wait_recv()
+        sends[4].wait_recv()
+
+    place(2)
 
     for copy in bias_copies:
         copy.wait()
@@ -211,8 +245,7 @@
             scr[:, pl.ds(p, xl, stride=2), :] = y
         out[a] = scr[...].astype(jnp.bfloat16)
 
-    for copy in sends:
-        copy.wait_send()
+    each(lambda k: sends[k].wait_send())
     for copy in swaps:
         copy.wait_send()
 
@@ -224,8 +257,8 @@
     anywhere = pl.BlockSpec(memory_space=pl.ANY)
     return pl.pallas_call(
         kernel,
-        out_shape=jax.ShapeDtypeStruct((2, 2 * zl, 2 * xl, f), bf16),
-        in_specs=[anywhere] * 5,
+        out_shape=pltpu.VMEM((2, 2 * zl, 2 * xl, f), bf16),
+        in_specs=[pl.BlockSpec(memory_space=pltpu.HBM)] * 5,
         out_specs=pl.BlockSpec(memory_space=pltpu.VMEM),
         scratch_shapes=[
             pltpu.VMEM((3, 2, zl, xl, cs), bf16),
@@ -246,7 +279,7 @@
             pltpu.SemaphoreType.DMA((2,)),
         ],
         compiler_params=pltpu.CompilerParams(
-            collective_id=0, has_side_effects=True, vmem_limit_bytes=60 * 1024 * 1024
+            collective_id=0, has_side_effects=True, vmem_limit_bytes=62 * 1024 * 1024
         ),
         cost_estimate=pl.CostEstimate(
             flops=2_500_000_000, bytes_accessed=8_000_000, transcendentals=0

time: 29.9 us -> 20.5 us (0.69)
  Pallas kernels: 28.1 us -> 19.7 us
  local copies, waits for them, and re-layouts: 1.67 us -> 0.71 us
    pallas_call x1, Pallas kernels: 28.1 us -> 19.7 us  [local(): pl.pallas_call(kernel, out_shape=pltpu.VMEM((2, 2 * zl, 2 * xl, f), bf16)...]
    unnamed x1, local copies, waits for them, and re-layouts: 1.67 us -> 0.71 us
where the time goes in v2:
time: 20.5 us; the launch traced here: 20.4 us
  Pallas kernels  19.7 us (96%)
  local copies, waits for them, and re-layouts  0.71 us (3%)
    pallas_call x1, Pallas kernels, local(): pl.pallas_call(kernel, out_shape=pltpu.VMEM((2, 2 * zl, 2 * xl, f), bf16)...  19.7 us
    unnamed x1, local copies, waits for them, and re-layouts  0.71 us

profile of v2, /device:TPU:1, one launch (start us, length us, event | category | flops | bytes accessed | tf_op | source)
XLA Modules:
  0.0 20.4 jit_solution(8698532887450835947)
XLA Ops:
  0.0 19.7 %section.1 = bf16[2,16,32,128]{3,2,1,0:T(8,128)(2,1)S(1)} custom-call(bf16[1,8,16,160]{3,2,1,0:T(8,128)(2,1)} %coarse.1, bf16[128,20480]{1,0:T(8,128)(2,1)} %upw.1, bf16[128]{0:T(256)(128)(2,1)} %upb.1, bf16[27,128,256]{2,1,0:T(8,128)(2,1)} %mixw.1, bf16[128]{0:T(256)(128)(2,1)} %mixb.1), custom_call_target="tpu_custom_call" | custom-call | flops 2500000000 | bytes 8000000 | tf_op jit(solution)/shard_map/section/pallas_call | solution.py:258
  19.7 0.7 %copy.7 = bf16[2,16,32,128]{3,2,1,0:T(8,128)(2,1)} copy(bf16[2,16,32,128]{3,2,1,0:T(8,128)(2,1)S(1)} %section.1) | data formatting | bytes 524288

commit v3 on v2

--- a/solution.py
+++ b/solution.py
@@ -17,7 +17,7 @@
 
 def kernel(
     coarse, upw, upb, mixw, mixb, out,
-    cbuf, wup, wmix, ub, mb, xb, hid, scr,
+    own, cmain, ctail, wup, wmix, ub, mb, xb, hid, scr,
     up_sem, mix_sem, bias_sem, own_sem, send_sem, recv_sem, hsend, hrecv,
 ):
     tiles = lax.axis_size("tile")
@@ -55,8 +55,12 @@
         )
     )
 
-    own_copy = pltpu.make_async_copy(coarse.at[0], cbuf.at[1, c], own_sem)
-    own_copy.start()
+    own_copies = [
+        pltpu.make_async_copy(coarse.at[0], own, own_sem.at[0]),
+        pltpu.make_async_copy(coarse.at[0, :, :, 0:128], cmain.at[1, c], own_sem.at[1]),
+    ]
+    for copy in own_copies:
+        copy.start()
     bias_copies = [
         pltpu.make_async_copy(upb, ub, bias_sem.at[0]),
         pltpu.make_async_copy(mixb, mb, bias_sem.at[1]),
@@ -81,40 +85,64 @@
         copy.start()
         mix_copies.append(copy)
 
+    @pl.when(jnp.logical_not(has_left))
+    def _():
+        cmain[0] = jnp.zeros_like(cmain[0])
+        ctail[0] = jnp.zeros_like(ctail[0])
+
+    @pl.when(jnp.logical_not(has_right))
+    def _():
+        cmain[2] = jnp.zeros_like(cmain[2])
+        ctail[2] = jnp.zeros_like(ctail[2])
+
+    first = has_left.astype(jnp.int32)
+    last = has_right.astype(jnp.int32)
+    pl.semaphore_wait(barrier, 1 + 2 * first + 2 * last)
+    sends = [
+        [
+            pltpu.make_async_remote_copy(
+                src_ref=src,
+                dst_ref=dst,
+                send_sem=send_sem.at[part, k],
+                recv_sem=recv_sem.at[part, k],
+                device_id=dev,
+                device_id_type=MESH,
+            )
+            for part, (src, dst) in enumerate(
+                (
+                    (coarse.at[0, :, :, 0:128], cmain.at[slot, c]),
+                    (ctail.at[1, c], ctail.at[slot, c]),
+                )
+            )
+        ]
+        for k, (dev, slot) in enumerate(zip(targets, slots))
+    ]
+    each(lambda k: sends[k][0].start())
+    own_copies[0].wait()
+    tail = own[:, :, 128:cs].astype(jnp.float32)
+    for i in range(zl // 4):
+        ctail[1, c, i] = jnp.concatenate(
+            [tail[4 * i + j] for j in range(4)], axis=-1
+        ).astype(jnp.bfloat16)
+    each(lambda k: sends[k][1].start())
+
     xb[:, :, :, 0] = jnp.zeros_like(xb[:, :, :, 0])
     xb[:, :, :, zl + 1] = jnp.zeros_like(xb[:, :, :, zl + 1])
     hid[:, :, 0] = jnp.zeros_like(hid[:, :, 0])
     hid[:, :, 2 * zl + 1] = jnp.zeros_like(hid[:, :, 2 * zl + 1])
-
-    @pl.when(jnp.logical_not(has_left))
-    def _():
-        cbuf[0] = jnp.zeros_like(cbuf[0])
-
-    @pl.when(jnp.logical_not(has_right))
-    def _():
-        cbuf[2] = jnp.zeros_like(cbuf[2])
-
-    first = has_left.astype(jnp.int32)
-    last = has_right.astype(jnp.int32)
-    pl.semaphore_wait(barrier, 1 + 2 * first + 2 * last)
-    sends = [
-        pltpu.make_async_remote_copy(
-            src_ref=coarse.at[0],
-            dst_ref=cbuf.at[slot, c],
-            send_sem=send_sem.at[k],
-            recv_sem=recv_sem.at[k],
-            device_id=dev,
-            device_id_type=MESH,
-        )
-        for k, (dev, slot) in enumerate(zip(targets, slots))
-    ]
-    each(lambda k: sends[k].start())
     first = first.astype(jnp.float32)
     last = last.astype(jnp.float32)
 
     def place(slot):
-        x = cbuf[slot].astype(jnp.float32)
-        x = jnp.concatenate([x[0], x[1]], axis=-1)
+        parts = []
+        for half in (0, 1):
+            parts.append(cmain[slot, half].astype(jnp.float32))
+            packed = ctail[slot, half].astype(jnp.float32)
+            tails = [
+                packed[z // 4, :, (z % 4) * 32 : (z % 4) * 32 + 32] for z in range(zl)
+            ]
+            parts.append(jnp.stack(tails, axis=0))
+        x = jnp.concatenate(parts, axis=-1)
         gap = jnp.zeros((zl, xl, 64), jnp.float32)
         edge = jnp.zeros((zl, 1, cin + 64), jnp.float32)
         for v, parts in enumerate(([gap, x], [x, gap])):
@@ -124,35 +152,34 @@
             for s, w in enumerate((low, y, high)):
                 xb[v, s, slot, 1 : zl + 1] = w.astype(jnp.bfloat16)
 
-    own_copy.wait()
-    sends[0].wait_recv()
+    def arrived(*which):
+        for k in which:
+            sends[k][0].wait_recv()
+            sends[k][1].wait_recv()
+
+    own_copies[1].wait()
+    arrived(0)
     place(1)
 
-    @pl.when(has_left)
-    def _():
-        sends[1].wait_recv()
-        sends[2].wait_recv()
-
-    place(0)
-
-    @pl.when(has_right)
-    def _():
-        sends[3].wait_recv()
-        sends[4].wait_recv()
-
-    place(2)
-
-    for copy in bias_copies:
+    for copy in (*bias_copies, *up_copies.values(), *mix_copies):
         copy.wait()
     ubias = ub[...].astype(jnp.float32).reshape(1, 1, 1, f)
     mbias = mb[...].astype(jnp.float32).reshape(1, f)
 
+    @pl.when(has_left)
+    def _():
+        arrived(1, 2)
+
+    @pl.when(has_right)
+    def _():
+        arrived(3, 4)
+
+    place(0)
+    place(2)
+
     m = 2 * zl * xl
     swaps = []
     for px in (0, 1):
-        for _, kx in TAPS[px]:
-            for ky in range(4):
-                up_copies[ky, kx].wait()
         for pz in (0, 1):
             lhs, even, odd = [], [], []
             for yt in (0, 1):
@@ -221,7 +248,6 @@
         left_side = jnp.concatenate([jnp.concatenate(g, axis=1) for g in lhs], axis=0)
         return dot_nt(left_side, rhs)
 
-    mix_copies[0].wait()
     total = mix(0)
     for copy in swaps:
         copy.wait_recv()
@@ -235,7 +261,6 @@
                 moved = jnp.concatenate([h[:, 1:], edge], axis=1)
             lane = 0 if px else 3 * f
             hid[1, r, 1 : 2 * zl + 1, :, lane : lane + f] = moved.astype(jnp.bfloat16)
-    mix_copies[1].wait()
     total = total + mix(1)
 
     for a in (0, 1):
@@ -245,7 +270,7 @@
             scr[:, pl.ds(p, xl, stride=2), :] = y
         out[a] = scr[...].astype(jnp.bfloat16)
 
-    each(lambda k: sends[k].wait_send())
+    each(lambda k: (sends[k][0].wait_send(), sends[k][1].wait_send()))
     for copy in swaps:
         copy.wait_send()
 
@@ -261,7 +286,9 @@
         in_specs=[pl.BlockSpec(memory_space=pltpu.HBM)] * 5,
         out_specs=pl.BlockSpec(memory_space=pltpu.VMEM),
         scratch_shapes=[
-            pltpu.VMEM((3, 2, zl, xl, cs), bf16),
+            pltpu.VMEM((zl, xl, cs), bf16),
+            pltpu.VMEM((3, 2, zl, xl, 128), bf16),
+            pltpu.VMEM((3, 2, zl // 4, xl, 128), bf16),
             pltpu.VMEM(up_weight.shape, bf16),
             pltpu.VMEM((2, 27, f, f), bf16),
             pltpu.VMEM((f,), bf16),
@@ -272,9 +299,9 @@
             pltpu.SemaphoreType.DMA((16,)),
             pltpu.SemaphoreType.DMA((2,)),
             pltpu.SemaphoreType.DMA((2,)),
-            pltpu.SemaphoreType.DMA,
-            pltpu.SemaphoreType.DMA((5,)),
-            pltpu.SemaphoreType.DMA((5,)),
+            pltpu.SemaphoreType.DMA((2,)),
+            pltpu.SemaphoreType.DMA((2, 5)),
+            pltpu.SemaphoreType.DMA((2, 5)),
             pltpu.SemaphoreType.DMA((2,)),
             pltpu.SemaphoreType.DMA((2,)),
         ],

time: 20.5 us -> 19.7 us (0.961)
  Pallas kernels: 19.7 us -> 18.9 us
    pallas_call x1, Pallas kernels: 19.7 us -> 18.9 us  [local(): pl.pallas_call(kernel, out_shape=pltpu.VMEM((2, 2 * zl, 2 * xl, f), bf16)...]
where the time goes in v3:
time: 19.7 us; the launch traced here: 19.6 us
  Pallas kernels  18.9 us (96%)
  local copies, waits for them, and re-layouts  0.71 us (4%)
    pallas_call x1, Pallas kernels, local(): pl.pallas_call(kernel, out_shape=pltpu.VMEM((2, 2 * zl, 2 * xl, f), bf16)...  18.9 us
    unnamed x1, local copies, waits for them, and re-layouts  0.71 us

profile of v3, /device:TPU:1, one launch (start us, length us, event | category | flops | bytes accessed | tf_op | source)
XLA Modules:
  0.0 19.6 jit_solution(17579775488706477685)
XLA Ops:
  0.0 18.9 %section.1 = bf16[2,16,32,128]{3,2,1,0:T(8,128)(2,1)S(1)} custom-call(bf16[1,8,16,160]{3,2,1,0:T(8,128)(2,1)} %coarse.1, bf16[128,20480]{1,0:T(8,128)(2,1)} %upw.1, bf16[128]{0:T(256)(128)(2,1)} %upb.1, bf16[27,128,256]{2,1,0:T(8,128)(2,1)} %mixw.1, bf16[128]{0:T(256)(128)(2,1)} %mixb.1), custom_call_target="tpu_custom_call" | custom-call | flops 2500000000 | bytes 8000000 | tf_op jit(solution)/shard_map/section/pallas_call | solution.py:283
  18.9 0.7 %copy.7 = bf16[2,16,32,128]{3,2,1,0:T(8,128)(2,1)} copy(bf16[2,16,32,128]{3,2,1,0:T(8,128)(2,1)S(1)} %section.1) | data formatting | bytes 524288

commit v4 on v3

--- a/solution.py
+++ b/solution.py
@@ -17,8 +17,8 @@
 
 def kernel(
     coarse, upw, upb, mixw, mixb, out,
-    own, cmain, ctail, wup, wmix, ub, mb, xb, hid, scr,
-    up_sem, mix_sem, bias_sem, own_sem, send_sem, recv_sem, hsend, hrecv,
+    own, cmain, ctail, wup, wmix, ub, mb, xb, hid, scr, acc,
+    up_sem, mix_sem, bias_sem, own_sem, send_sem, recv_sem, hand_send, hand_recv, hsend, hrecv,
 ):
     tiles = lax.axis_size("tile")
     t = lax.axis_index("tile")
@@ -35,24 +35,33 @@
     has_left = t > 0
     has_right = t < tiles - 1
 
-    def each(action):
+    corner = jnp.logical_and(t == 0, c == 0)
+    hands_on = jnp.logical_and(t == 0, c == 1)
+
+    def each(action, to_right, to_left):
         action(0)
 
-        @pl.when(has_right)
+        @pl.when(to_right)
         def _():
             action(1)
             action(2)
 
-        @pl.when(has_left)
-        def _():
-            action(3)
-            action(4)
+        for k, core in ((3, c), (4, other)):
+
+            @pl.when(to_left(core))
+            def _(k=k):
+                action(k)
+
+    def sends_left(core):
+        return jnp.logical_or(t > 1, jnp.logical_and(t == 1, core == 1))
 
     barrier = pltpu.get_barrier_semaphore()
     each(
         lambda k: pl.semaphore_signal(
             barrier, inc=1, device_id=targets[k], device_id_type=MESH
-        )
+        ),
+        jnp.logical_and(has_right, jnp.logical_not(corner)),
+        lambda core: has_left,
     )
 
     own_copies = [
@@ -97,7 +106,7 @@
 
     first = has_left.astype(jnp.int32)
     last = has_right.astype(jnp.int32)
-    pl.semaphore_wait(barrier, 1 + 2 * first + 2 * last)
+    pl.semaphore_wait(barrier, 1 + 2 * first + 2 * last - (t == 1).astype(jnp.int32))
     sends = [
         [
             pltpu.make_async_remote_copy(
@@ -117,14 +126,37 @@
         ]
         for k, (dev, slot) in enumerate(zip(targets, slots))
     ]
-    each(lambda k: sends[k][0].start())
+    each(lambda k: sends[k][0].start(), has_right, sends_left)
     own_copies[0].wait()
     tail = own[:, :, 128:cs].astype(jnp.float32)
     for i in range(zl // 4):
         ctail[1, c, i] = jnp.concatenate(
             [tail[4 * i + j] for j in range(4)], axis=-1
         ).astype(jnp.bfloat16)
-    each(lambda k: sends[k][1].start())
+    each(lambda k: sends[k][1].start(), has_right, sends_left)
+
+    handed = [
+        pltpu.make_async_remote_copy(
+            src_ref=buf.at[2],
+            dst_ref=buf.at[2],
+            send_sem=hand_send.at[part],
+            recv_sem=hand_recv.at[part],
+            device_id=(t, other),
+            device_id_type=MESH,
+        )
+        for part, buf in enumerate((cmain, ctail))
+    ]
+
+    def arrived(*which):
+        for k in which:
+            sends[k][0].wait_recv()
+            sends[k][1].wait_recv()
+
+    @pl.when(hands_on)
+    def _():
+        arrived(3, 4)
+        for copy in handed:
+            copy.start()
 
     xb[:, :, :, 0] = jnp.zeros_like(xb[:, :, :, 0])
     xb[:, :, :, zl + 1] = jnp.zeros_like(xb[:, :, :, zl + 1])
@@ -152,16 +184,11 @@
             for s, w in enumerate((low, y, high)):
                 xb[v, s, slot, 1 : zl + 1] = w.astype(jnp.bfloat16)
 
-    def arrived(*which):
-        for k in which:
-            sends[k][0].wait_recv()
-            sends[k][1].wait_recv()
-
     own_copies[1].wait()
     arrived(0)
     place(1)
 
-    for copy in (*bias_copies, *up_copies.values(), *mix_copies):
+    for copy in (*bias_copies, *[up_copies[ky, kx] for ky in range(4) for kx in (1, 3)]):
         copy.wait()
     ubias = ub[...].astype(jnp.float32).reshape(1, 1, 1, f)
     mbias = mb[...].astype(jnp.float32).reshape(1, f)
@@ -170,9 +197,14 @@
     def _():
         arrived(1, 2)
 
-    @pl.when(has_right)
+    @pl.when(jnp.logical_and(has_right, t > 0))
     def _():
         arrived(3, 4)
+
+    @pl.when(corner)
+    def _():
+        for copy in handed:
+            copy.wait_recv()
 
     place(0)
     place(2)
@@ -180,6 +212,9 @@
     m = 2 * zl * xl
     swaps = []
     for px in (0, 1):
+        if px:
+            for copy in (*[up_copies[ky, kx] for ky in range(4) for kx in (0, 2)], *mix_copies):
+                copy.wait()
         for pz in (0, 1):
             lhs, even, odd = [], [], []
             for yt in (0, 1):
@@ -248,7 +283,10 @@
         left_side = jnp.concatenate([jnp.concatenate(g, axis=1) for g in lhs], axis=0)
         return dot_nt(left_side, rhs)
 
-    total = mix(0)
+    @pl.when(c >= 0)
+    def _():
+        acc[...] = mix(0)
+
     for copy in swaps:
         copy.wait_recv()
     for px in (0, 1):
@@ -261,7 +299,7 @@
                 moved = jnp.concatenate([h[:, 1:], edge], axis=1)
             lane = 0 if px else 3 * f
             hid[1, r, 1 : 2 * zl + 1, :, lane : lane + f] = moved.astype(jnp.bfloat16)
-    total = total + mix(1)
+    total = acc[...] + mix(1)
 
     for a in (0, 1):
         for p in (0, 1):
@@ -270,7 +308,15 @@
             scr[:, pl.ds(p, xl, stride=2), :] = y
         out[a] = scr[...].astype(jnp.bfloat16)
 
-    each(lambda k: (sends[k][0].wait_send(), sends[k][1].wait_send()))
+    each(
+        lambda k: (sends[k][0].wait_send(), sends[k][1].wait_send()), has_right, sends_left
+    )
+
+    @pl.when(hands_on)
+    def _():
+        for copy in handed:
+            copy.wait_send()
+
     for copy in swaps:
         copy.wait_send()
 
@@ -296,12 +342,15 @@
             pltpu.VMEM((2, 3, 3, zl + 2, xl, 2 * cs + 64), bf16),
             pltpu.VMEM((2, 4, 2 * zl + 2, xl, 4 * f), bf16),
             pltpu.VMEM((2 * zl, 2 * xl, f), jnp.float32),
+            pltpu.VMEM((4 * zl * xl, 2 * f), jnp.float32),
             pltpu.SemaphoreType.DMA((16,)),
             pltpu.SemaphoreType.DMA((2,)),
             pltpu.SemaphoreType.DMA((2,)),
             pltpu.SemaphoreType.DMA((2,)),
             pltpu.SemaphoreType.DMA((2, 5)),
             pltpu.SemaphoreType.DMA((2, 5)),
+            pltpu.SemaphoreType.DMA((2,)),
+            pltpu.SemaphoreType.DMA((2,)),
             pltpu.SemaphoreType.DMA((2,)),
             pltpu.SemaphoreType.DMA((2,)),
         ],

time: 19.7 us -> 17.8 us (0.904)
  the two profiles are of different devices: /device:TPU:1 before, /device:TPU:255 now
where the time goes in v4:
time: 17.8 us; the launch traced here: 17.7 us
  Pallas kernels  17 us (96%)
  local copies, waits for them, and re-layouts  0.71 us (4%)
    pallas_call x1, Pallas kernels, local(): pl.pallas_call(kernel, out_shape=pltpu.VMEM((2, 2 * zl, 2 * xl, f), bf16)...  17 us
    unnamed x1, local copies, waits for them, and re-layouts  0.71 us

profile of v4, /device:TPU:255, one launch (start us, length us, event | category | flops | bytes accessed | tf_op | source)
XLA Modules:
  0.0 17.7 jit_solution(14315083881807894855)
XLA Ops:
  0.0 17.0 %section.1 = bf16[2,16,32,128]{3,2,1,0:T(8,128)(2,1)S(1)} custom-call(bf16[1,8,16,160]{3,2,1,0:T(8,128)(2,1)} %coarse.1, bf16[128,20480]{1,0:T(8,128)(2,1)} %upw.1, bf16[128]{0:T(256)(128)(2,1)} %upb.1, bf16[27,128,256]{2,1,0:T(8,128)(2,1)} %mixw.1, bf16[128]{0:T(256)(128)(2,1)} %mixb.1), custom_call_target="tpu_custom_call" | custom-call | flops 2500000000 | bytes 8000000 | tf_op jit(solution)/shard_map/section/pallas_call | solution.py:329
  17.0 0.7 %copy.7 = bf16[2,16,32,128]{3,2,1,0:T(8,128)(2,1)} copy(bf16[2,16,32,128]{3,2,1,0:T(8,128)(2,1)S(1)} %section.1) | data formatting | bytes 524288

commit v5 on v4

--- a/solution.py
+++ b/solution.py
@@ -39,8 +39,6 @@
     hands_on = jnp.logical_and(t == 0, c == 1)
 
     def each(action, to_right, to_left):
-        action(0)
-
         @pl.when(to_right)
         def _():
             action(1)
@@ -51,6 +49,8 @@
             @pl.when(to_left(core))
             def _(k=k):
                 action(k)
+
+        action(0)
 
     def sends_left(core):
         return jnp.logical_or(t > 1, jnp.logical_and(t == 1, core == 1))
@@ -74,25 +74,22 @@
         pltpu.make_async_copy(upb, ub, bias_sem.at[0]),
         pltpu.make_async_copy(mixb, mb, bias_sem.at[1]),
     ]
-    for copy in bias_copies:
-        copy.start()
     up_copies = {}
-    for px in (0, 1):
-        for _, kx in TAPS[px]:
-            for ky in range(4):
-                cols = pl.ds((16 * ky + 4 * kx) * cin, 4 * cin)
-                copy = pltpu.make_async_copy(
-                    upw.at[:, cols], wup.at[:, cols], up_sem.at[4 * ky + kx]
-                )
-                copy.start()
-                up_copies[ky, kx] = copy
-    mix_copies = []
-    for half, src in ((0, c), (1, other)):
-        copy = pltpu.make_async_copy(
+    for kx in range(4):
+        for ky in range(4):
+            cols = pl.ds((16 * ky + 4 * kx) * cin, 4 * cin)
+            up_copies[ky, kx] = pltpu.make_async_copy(
+                upw.at[:, cols], wup.at[:, cols], up_sem.at[4 * ky + kx]
+            )
+    up_groups = [[up_copies[ky, kx] for _, kx in TAPS[px] for ky in range(4)] for px in (0, 1)]
+    mix_copies = [
+        pltpu.make_async_copy(
             mixw.at[:, :, pl.ds(pl.multiple_of(src * f, f), f)], wmix.at[half], mix_sem.at[half]
         )
+        for half, src in ((0, c), (1, other))
+    ]
+    for copy in up_groups[0]:
         copy.start()
-        mix_copies.append(copy)
 
     @pl.when(jnp.logical_not(has_left))
     def _():
@@ -127,6 +124,9 @@
         for k, (dev, slot) in enumerate(zip(targets, slots))
     ]
     each(lambda k: sends[k][0].start(), has_right, sends_left)
+    for copy in (*up_groups[1], *mix_copies, *bias_copies):
+        copy.start()
+
     own_copies[0].wait()
     tail = own[:, :, 128:cs].astype(jnp.float32)
     for i in range(zl // 4):
@@ -262,30 +262,48 @@
         copy.start()
         swaps.append(copy)
 
+    def window(half, r, dz, xs):
+        lanes = slice(xs[0] * f, (xs[-1] + 1) * f)
+        return hid[half, r, dz : dz + 2 * zl, :, lanes].reshape(m, len(xs) * f)
+
+    def tap(half, a, p, r, x, dz):
+        dy, dx = r - a, x - p
+        if 0 <= dy < 3 and 0 <= dx < 3:
+            return wmix[half, 9 * dy + 3 * dx + dz]
+        return jnp.zeros((f, f), jnp.bfloat16)
+
+    groups = (
+        ((1, 2), (1, 2), ((0, 0), (0, 1), (1, 0), (1, 1))),
+        ((0,), (1, 2), ((0, 0), (0, 1))),
+        ((3,), (1, 2), ((1, 0), (1, 1))),
+        ((0, 1, 2, 3), (0,), ((0, 0), (1, 0))),
+        ((0, 1, 2, 3), (3,), ((0, 1), (1, 1))),
+    )
+
     def mix(half):
-        lhs = [[], []]
-        groups = [[], []]
-        blank = jnp.zeros((f, 3 * f), jnp.bfloat16)
-        for r in range(4):
-            for dz in range(3):
-                for p in (0, 1):
-                    lhs[p].append(
-                        hid[half, r, dz : dz + 2 * zl, :, p * f : (p + 3) * f].reshape(m, 3 * f)
+        parts = {}
+        for rows, xs, outs in groups:
+            steps = [(r, dz) for r in rows for dz in range(3)]
+            lhs = jnp.concatenate([window(half, r, dz, xs) for r, dz in steps], axis=1)
+            rhs = jnp.concatenate(
+                [
+                    jnp.concatenate(
+                        [tap(half, a, p, r, x, dz) for r, dz in steps for x in xs], axis=1
                     )
-                for a in (0, 1):
-                    dy = r - a
-                    if 0 <= dy < 3:
-                        taps = [wmix[half, 9 * dy + 3 * dx + dz] for dx in range(3)]
-                        groups[a].append(jnp.concatenate(taps, axis=1))
-                    else:
-                        groups[a].append(blank)
-        rhs = jnp.concatenate([jnp.concatenate(g, axis=1) for g in groups], axis=0)
-        left_side = jnp.concatenate([jnp.concatenate(g, axis=1) for g in lhs], axis=0)
-        return dot_nt(left_side, rhs)
+                    for a, p in outs
+                ],
+                axis=0,
+            )
+            got = dot_nt(lhs, rhs)
+            for i, key in enumerate(outs):
+                part = got[:, i * f : (i + 1) * f]
+                parts[key] = parts[key] + part if key in parts else part
+        return parts
 
     @pl.when(c >= 0)
     def _():
-        acc[...] = mix(0)
+        for (a, p), part in mix(0).items():
+            acc[a, p] = part
 
     for copy in swaps:
         copy.wait_recv()
@@ -299,11 +317,11 @@
                 moved = jnp.concatenate([h[:, 1:], edge], axis=1)
             lane = 0 if px else 3 * f
             hid[1, r, 1 : 2 * zl + 1, :, lane : lane + f] = moved.astype(jnp.bfloat16)
-    total = acc[...] + mix(1)
+    rest = mix(1)
 
     for a in (0, 1):
         for p in (0, 1):
-            y = total[p * m : (p + 1) * m, a * f : (a + 1) * f] + mbias
+            y = acc[a, p] + rest[a, p] + mbias
             y = jnp.maximum(y, 0.0).reshape(2 * zl, xl, f)
             scr[:, pl.ds(p, xl, stride=2), :] = y
         out[a] = scr[...].astype(jnp.bfloat16)
@@ -342,7 +360,7 @@
             pltpu.VMEM((2, 3, 3, zl + 2, xl, 2 * cs + 64), bf16),
             pltpu.VMEM((2, 4, 2 * zl + 2, xl, 4 * f), bf16),
             pltpu.VMEM((2 * zl, 2 * xl, f), jnp.float32),
-            pltpu.VMEM((4 * zl * xl, 2 * f), jnp.float32),
+            pltpu.VMEM((2, 2, 2 * zl * xl, f), jnp.float32),
             pltpu.SemaphoreType.DMA((16,)),
             pltpu.SemaphoreType.DMA((2,)),
             pltpu.SemaphoreType.DMA((2,)),

time: 17.8 us -> 17.6 us (0.989)
  Pallas kernels: 17 us -> 16.8 us
where the time goes in v5:
time: 17.6 us; the launch traced here: 17.5 us
  Pallas kernels  16.8 us (95%)
  local copies, waits for them, and re-layouts  0.71 us (4%)
    pallas_call x1, Pallas kernels, local(): pl.pallas_call(kernel, out_shape=pltpu.VMEM((2, 2 * zl, 2 * xl, f), bf16)...  16.8 us
    unnamed x1, local copies, waits for them, and re-layouts  0.71 us

profile of v5, /device:TPU:255, one launch (start us, length us, event | category | flops | bytes accessed | tf_op | source)
XLA Modules:
  0.0 17.5 jit_solution(15649015218456585289)
XLA Ops:
  0.0 16.8 %section.1 = bf16[2,16,32,128]{3,2,1,0:T(8,128)(2,1)S(1)} custom-call(bf16[1,8,16,160]{3,2,1,0:T(8,128)(2,1)} %coarse.1, bf16[128,20480]{1,0:T(8,128)(2,1)} %upw.1, bf16[128]{0:T(256)(128)(2,1)} %upb.1, bf16[27,128,256]{2,1,0:T(8,128)(2,1)} %mixw.1, bf16[128]{0:T(256)(128)(2,1)} %mixb.1), custom_call_target="tpu_custom_call" | custom-call | flops 2500000000 | bytes 8000000 | tf_op jit(solution)/shard_map/section/pallas_call | solution.py:347
  16.8 0.7 %copy.7 = bf16[2,16,32,128]{3,2,1,0:T(8,128)(2,1)} copy(bf16[2,16,32,128]{3,2,1,0:T(8,128)(2,1)S(1)} %section.1) | data formatting | bytes 524288

commit v6 on v5

--- a/solution.py
+++ b/solution.py
@@ -15,9 +15,13 @@
     return lax.dot_general(a, b, NT, preferred_element_type=jnp.float32)
 
 
+def side_by_side(ref, at, cin):
+    return jnp.concatenate([ref[:, s : s + cin] for s in at], axis=1)
+
+
 def kernel(
     coarse, upw, upb, mixw, mixb, out,
-    own, cmain, ctail, wup, wmix, ub, mb, xb, hid, scr, acc,
+    own, cmain, ctail, wup, wd, wmix, ub, mb, xb, hid, scr, acc,
     up_sem, mix_sem, bias_sem, own_sem, send_sem, recv_sem, hand_send, hand_recv, hsend, hrecv,
 ):
     tiles = lax.axis_size("tile")
@@ -103,6 +107,16 @@
 
     first = has_left.astype(jnp.int32)
     last = has_right.astype(jnp.int32)
+    @pl.when(c >= 0)
+    def _():
+        own_copies[1].wait()
+        own_copies[0].wait()
+        tail = own[:, :, 128:cs].astype(jnp.float32)
+        for i in range(zl // 4):
+            ctail[1, c, i] = jnp.concatenate(
+                [tail[4 * i + j] for j in range(4)], axis=-1
+            ).astype(jnp.bfloat16)
+
     pl.semaphore_wait(barrier, 1 + 2 * first + 2 * last - (t == 1).astype(jnp.int32))
     sends = [
         [
@@ -116,7 +130,7 @@
             )
             for part, (src, dst) in enumerate(
                 (
-                    (coarse.at[0, :, :, 0:128], cmain.at[slot, c]),
+                    (cmain.at[1, c], cmain.at[slot, c]),
                     (ctail.at[1, c], ctail.at[slot, c]),
                 )
             )
@@ -127,12 +141,6 @@
     for copy in (*up_groups[1], *mix_copies, *bias_copies):
         copy.start()
 
-    own_copies[0].wait()
-    tail = own[:, :, 128:cs].astype(jnp.float32)
-    for i in range(zl // 4):
-        ctail[1, c, i] = jnp.concatenate(
-            [tail[4 * i + j] for j in range(4)], axis=-1
-        ).astype(jnp.bfloat16)
     each(lambda k: sends[k][1].start(), has_right, sends_left)
 
     handed = [
@@ -168,27 +176,45 @@
     def place(slot):
         parts = []
         for half in (0, 1):
-            parts.append(cmain[slot, half].astype(jnp.float32))
-            packed = ctail[slot, half].astype(jnp.float32)
+            parts.append(cmain[slot, half])
+            packed = ctail[slot, half]
             tails = [
                 packed[z // 4, :, (z % 4) * 32 : (z % 4) * 32 + 32] for z in range(zl)
             ]
             parts.append(jnp.stack(tails, axis=0))
         x = jnp.concatenate(parts, axis=-1)
-        gap = jnp.zeros((zl, xl, 64), jnp.float32)
+        gap = jnp.zeros((zl, xl, 64), jnp.bfloat16)
         edge = jnp.zeros((zl, 1, cin + 64), jnp.float32)
         for v, parts in enumerate(([gap, x], [x, gap])):
-            y = jnp.concatenate(parts, axis=-1)
+            y = jnp.concatenate(parts, axis=-1).astype(jnp.float32)
             low = jnp.concatenate([edge, y[:, :-1]], axis=1)
             high = jnp.concatenate([y[:, 1:], edge], axis=1)
             for s, w in enumerate((low, y, high)):
                 xb[v, s, slot, 1 : zl + 1] = w.astype(jnp.bfloat16)
 
-    own_copies[1].wait()
     arrived(0)
     place(1)
 
-    for copy in (*bias_copies, *[up_copies[ky, kx] for ky in range(4) for kx in (1, 3)]):
+    def pair(px, ky, kz):
+        return ((px * 4 + ky) * 4 + kz) * 2 * cin
+
+    def join(px):
+        (_, ka), (_, kb) = TAPS[px]
+        for ky in range(4):
+            for kz in range(4):
+                at = [(16 * ky + 4 * kx + kz) * cin for kx in (ka, kb)]
+                start = pair(px, ky, kz)
+                wd[:, start : start + 2 * cin] = side_by_side(wup, at, cin)
+
+    for px in (0, 1):
+        for copy in up_groups[px]:
+            copy.wait()
+
+        @pl.when(c >= 0)
+        def _(px=px):
+            join(px)
+
+    for copy in (*bias_copies, *mix_copies):
         copy.wait()
     ubias = ub[...].astype(jnp.float32).reshape(1, 1, 1, f)
     mbias = mb[...].astype(jnp.float32).reshape(1, f)
@@ -212,20 +238,18 @@
     m = 2 * zl * xl
     swaps = []
     for px in (0, 1):
-        if px:
-            for copy in (*[up_copies[ky, kx] for ky in range(4) for kx in (0, 2)], *mix_copies):
-                copy.wait()
         for pz in (0, 1):
             lhs, even, odd = [], [], []
             for yt in (0, 1):
                 for dz, kz in TAPS[pz]:
-                    for dx, kx in TAPS[px]:
-                        lhs.append(
-                            xb[pz, dx + 1, yt : yt + 2, dz + 1 : dz + 1 + zl].reshape(m, cin + 64)
-                        )
-                        for ky, group in ((2 - 2 * yt, even), (3 - 2 * yt, odd)):
-                            start = (16 * ky + 4 * kx + kz) * cin - (0 if pz else 64)
-                            group.append(wup[:, start : start + cin + 64])
+                    near, far = [
+                        xb[v, dx + 1, yt : yt + 2, dz + 1 : dz + 1 + zl].reshape(m, cin + 64)
+                        for v, (dx, _) in zip((1, 0), TAPS[px])
+                    ]
+                    lhs += [near[:, :256], near[:, 256:] + far[:, :128], far[:, 128:]]
+                    for ky, group in ((2 - 2 * yt, even), (3 - 2 * yt, odd)):
+                        start = pair(px, ky, kz)
+                        group.append(wd[:, start : start + 2 * cin])
             rhs = jnp.concatenate(
                 [jnp.concatenate(even, axis=1), jnp.concatenate(odd, axis=1)], axis=0
             )
@@ -354,6 +378,7 @@
             pltpu.VMEM((3, 2, zl, xl, 128), bf16),
             pltpu.VMEM((3, 2, zl // 4, xl, 128), bf16),
             pltpu.VMEM(up_weight.shape, bf16),
+            pltpu.VMEM(up_weight.shape, bf16),
             pltpu.VMEM((2, 27, f, f), bf16),
             pltpu.VMEM((f,), bf16),
             pltpu.VMEM((f,), bf16),

time: 17.6 us -> 17.2 us (0.977)
  the two profiles are of different devices: /device:TPU:255 before, /device:TPU:1 now
where the time goes in v6:
time: 17.2 us; the launch traced here: 17 us
  Pallas kernels  16.3 us (95%)
  local copies, waits for them, and re-layouts  0.71 us (4%)
    pallas_call x1, Pallas kernels, local(): pl.pallas_call(kernel, out_shape=pltpu.VMEM((2, 2 * zl, 2 * xl, f), bf16)...  16.3 us
    unnamed x1, local copies, waits for them, and re-layouts  0.71 us

profile of v6, /device:TPU:1, one launch (start us, length us, event | category | flops | bytes accessed | tf_op | source)
XLA Modules:
  0.0 17.0 jit_solution(16669053725795774977)
XLA Ops:
  0.0 16.3 %section.1 = bf16[2,16,32,128]{3,2,1,0:T(8,128)(2,1)S(1)} custom-call(bf16[1,8,16,160]{3,2,1,0:T(8,128)(2,1)} %coarse.1, bf16[128,20480]{1,0:T(8,128)(2,1)} %upw.1, bf16[128]{0:T(256)(128)(2,1)} %upb.1, bf16[27,128,256]{2,1,0:T(8,128)(2,1)} %mixw.1, bf16[128]{0:T(256)(128)(2,1)} %mixb.1), custom_call_target="tpu_custom_call" | custom-call | flops 2500000000 | bytes 8000000 | tf_op jit(solution)/shard_map/section/pallas_call | solution.py:371
  16.3 0.7 %copy.7 = bf16[2,16,32,128]{3,2,1,0:T(8,128)(2,1)} copy(bf16[2,16,32,128]{3,2,1,0:T(8,128)(2,1)S(1)} %section.1) | data formatting | bytes 524288

commit v7 on v6

--- a/solution.py
+++ b/solution.py
@@ -92,8 +92,11 @@
         )
         for half, src in ((0, c), (1, other))
     ]
-    for copy in up_groups[0]:
-        copy.start()
+
+    @pl.when(corner)
+    def _():
+        for copy in (*up_groups[0], *up_groups[1], *mix_copies, *bias_copies):
+            copy.start()
 
     @pl.when(jnp.logical_not(has_left))
     def _():
@@ -116,6 +119,11 @@
             ctail[1, c, i] = jnp.concatenate(
                 [tail[4 * i + j] for j in range(4)], axis=-1
             ).astype(jnp.bfloat16)
+
+    @pl.when(jnp.logical_not(corner))
+    def _():
+        for copy in up_groups[0]:
+            copy.start()
 
     pl.semaphore_wait(barrier, 1 + 2 * first + 2 * last - (t == 1).astype(jnp.int32))
     sends = [
@@ -138,8 +146,12 @@
         for k, (dev, slot) in enumerate(zip(targets, slots))
     ]
     each(lambda k: sends[k][0].start(), has_right, sends_left)
-    for copy in (*up_groups[1], *mix_copies, *bias_copies):
-        copy.start()
+
+    @pl.when(jnp.logical_not(corner))
+    def _():
+        for copy in (*up_groups[1], *mix_copies, *bias_copies):
+            copy.start()
+
 
     each(lambda k: sends[k][1].start(), has_right, sends_left)
 
@@ -304,7 +316,7 @@
         ((0, 1, 2, 3), (3,), ((0, 1), (1, 1))),
     )
 
-    def mix(half):
+    def mix(half, groups):
         parts = {}
         for rows, xs, outs in groups:
             steps = [(r, dz) for r in rows for dz in range(3)]
@@ -326,12 +338,10 @@
 
     @pl.when(c >= 0)
     def _():
-        for (a, p), part in mix(0).items():
+        for (a, p), part in mix(0, groups).items():
             acc[a, p] = part
 
-    for copy in swaps:
-        copy.wait_recv()
-    for px in (0, 1):
+    def widen(px):
         for r in range(4):
             h = hid[1, r, 1 : 2 * zl + 1, :, (1 + px) * f : (2 + px) * f].astype(jnp.float32)
             edge = jnp.zeros((2 * zl, 1, f), jnp.float32)
@@ -341,7 +351,18 @@
                 moved = jnp.concatenate([h[:, 1:], edge], axis=1)
             lane = 0 if px else 3 * f
             hid[1, r, 1 : 2 * zl + 1, :, lane : lane + f] = moved.astype(jnp.bfloat16)
-    rest = mix(1)
+
+    swaps[0].wait_recv()
+
+    @pl.when(c >= 0)
+    def _():
+        widen(0)
+        for (a, p), part in mix(1, groups[-1:]).items():
+            acc[a, p] += part
+
+    swaps[1].wait_recv()
+    widen(1)
+    rest = mix(1, groups[:-1])
 
     for a in (0, 1):
         for p in (0, 1):

time: 17.2 us -> 18.1 us (1.052)
  Pallas kernels: 16.3 us -> 17.3 us
    pallas_call x1, Pallas kernels: 16.3 us -> 17.3 us  [local(): pl.pallas_call(kernel, out_shape=pltpu.VMEM((2, 2 * zl, 2 * xl, f), bf16)...]
where the time goes in v7:
time: 18.1 us; the launch traced here: 18 us
  Pallas kernels  17.3 us (96%)
  local copies, waits for them, and re-layouts  0.71 us (4%)
    pallas_call x1, Pallas kernels, local(): pl.pallas_call(kernel, out_shape=pltpu.VMEM((2, 2 * zl, 2 * xl, f), bf16)...  17.3 us
    unnamed x1, local copies, waits for them, and re-layouts  0.71 us

profile of v7, /device:TPU:1, one launch (start us, length us, event | category | flops | bytes accessed | tf_op | source)
XLA Modules:
  0.0 18.0 jit_solution(8544557367455739456)
XLA Ops:
  0.0 17.3 %section.1 = bf16[2,16,32,128]{3,2,1,0:T(8,128)(2,1)S(1)} custom-call(bf16[1,8,16,160]{3,2,1,0:T(8,128)(2,1)} %coarse.1, bf16[128,20480]{1,0:T(8,128)(2,1)} %upw.1, bf16[128]{0:T(256)(128)(2,1)} %upb.1, bf16[27,128,256]{2,1,0:T(8,128)(2,1)} %mixw.1, bf16[128]{0:T(256)(128)(2,1)} %mixb.1), custom_call_target="tpu_custom_call" | custom-call | flops 2500000000 | bytes 8000000 | tf_op jit(solution)/shard_map/section/pallas_call | solution.py:392
  17.3 0.7 %copy.7 = bf16[2,16,32,128]{3,2,1,0:T(8,128)(2,1)} copy(bf16[2,16,32,128]{3,2,1,0:T(8,128)(2,1)S(1)} %section.1) | data formatting | bytes 524288

commit v8 on v7

--- a/solution.py
+++ b/solution.py
@@ -93,11 +93,6 @@
         for half, src in ((0, c), (1, other))
     ]
 
-    @pl.when(corner)
-    def _():
-        for copy in (*up_groups[0], *up_groups[1], *mix_copies, *bias_copies):
-            copy.start()
-
     @pl.when(jnp.logical_not(has_left))
     def _():
         cmain[0] = jnp.zeros_like(cmain[0])
@@ -120,11 +115,8 @@
                 [tail[4 * i + j] for j in range(4)], axis=-1
             ).astype(jnp.bfloat16)
 
-    @pl.when(jnp.logical_not(corner))
-    def _():
-        for copy in up_groups[0]:
-            copy.start()
-
+    for copy in up_groups[0]:
+        copy.start()
     pl.semaphore_wait(barrier, 1 + 2 * first + 2 * last - (t == 1).astype(jnp.int32))
     sends = [
         [
@@ -146,12 +138,8 @@
         for k, (dev, slot) in enumerate(zip(targets, slots))
     ]
     each(lambda k: sends[k][0].start(), has_right, sends_left)
-
-    @pl.when(jnp.logical_not(corner))
-    def _():
-        for copy in (*up_groups[1], *mix_copies, *bias_copies):
-            copy.start()
-
+    for copy in (*bias_copies, *up_groups[1], *mix_copies):
+        copy.start()
 
     each(lambda k: sends[k][1].start(), has_right, sends_left)
 
@@ -218,15 +206,20 @@
                 start = pair(px, ky, kz)
                 wd[:, start : start + 2 * cin] = side_by_side(wup, at, cin)
 
-    for px in (0, 1):
+    def ready(px):
         for copy in up_groups[px]:
             copy.wait()
-
-        @pl.when(c >= 0)
-        def _(px=px):
-            join(px)
-
-    for copy in (*bias_copies, *mix_copies):
+        join(px)
+
+    @pl.when(c >= 0)
+    def _():
+        ready(0)
+
+    @pl.when(jnp.logical_not(corner))
+    def _():
+        ready(1)
+
+    for copy in bias_copies:
         copy.wait()
     ubias = ub[...].astype(jnp.float32).reshape(1, 1, 1, f)
     mbias = mb[...].astype(jnp.float32).reshape(1, f)
@@ -250,6 +243,12 @@
     m = 2 * zl * xl
     swaps = []
     for px in (0, 1):
+        if px:
+
+            @pl.when(corner)
+            def _():
+                ready(1)
+
         for pz in (0, 1):
             lhs, even, odd = [], [], []
             for yt in (0, 1):
@@ -336,6 +335,9 @@
                 parts[key] = parts[key] + part if key in parts else part
         return parts
 
+    for copy in mix_copies:
+        copy.wait()
+
     @pl.when(c >= 0)
     def _():
         for (a, p), part in mix(0, groups).items():

time: 18.1 us -> 17 us (0.939); the launches traced: 18 us -> 16.7 us
  Pallas kernels: 17.3 us -> 15.9 us
    pallas_call x1, Pallas kernels: 17.3 us -> 15.9 us  [local(): pl.pallas_call(kernel, out_shape=pltpu.VMEM((2, 2 * zl, 2 * xl, f), bf16)...]
where the time goes in v8:
time: 17 us; the launch traced here: 16.7 us
  Pallas kernels  15.9 us (94%)
  local copies, waits for them, and re-layouts  0.71 us (4%)
    pallas_call x1, Pallas kernels, local(): pl.pallas_call(kernel, out_shape=pltpu.VMEM((2, 2 * zl, 2 * xl, f), bf16)...  15.9 us
    unnamed x1, local copies, waits for them, and re-layouts  0.71 us

profile of v8, /device:TPU:1, one launch (start us, length us, event | category | flops | bytes accessed | tf_op | source)
XLA Modules:
  0.0 16.7 jit_solution(2298401671648440811)
XLA Ops:
  0.0 15.9 %section.1 = bf16[2,16,32,128]{3,2,1,0:T(8,128)(2,1)S(1)} custom-call(bf16[1,8,16,160]{3,2,1,0:T(8,128)(2,1)} %coarse.1, bf16[128,20480]{1,0:T(8,128)(2,1)} %upw.1, bf16[128]{0:T(256)(128)(2,1)} %upb.1, bf16[27,128,256]{2,1,0:T(8,128)(2,1)} %mixw.1, bf16[128]{0:T(256)(128)(2,1)} %mixb.1), custom_call_target="tpu_custom_call" | custom-call | flops 2500000000 | bytes 8000000 | tf_op jit(solution)/shard_map/section/pallas_call | solution.py:394
  15.9 0.7 %copy.7 = bf16[2,16,32,128]{3,2,1,0:T(8,128)(2,1)} copy(bf16[2,16,32,128]{3,2,1,0:T(8,128)(2,1)S(1)} %section.1) | data formatting | bytes 524288
